TPU v7x, 32 devices: a whole 2x2x4 slice. The times are simulated.
32 devices in a mesh: expert: 8 (over y, x, core), hidden: 4 (over z).
Axes of the slice: x: 2, y: 2, z: 4, core: 2. Of those that a mesh axis runs over, the one named last changes fastest.
Arguments:
- tokens: bfloat16 [16384, 1024], P(('expert', 'hidden')), may hold values from -6 to 6
- token_ids: int32 [16384], P(('expert', 'hidden')), may hold values from 0 to 8007, as said below
- hash_table: int32 [8008], replicated, may hold values from 0 to 15, as said below
- first_gain: float32 [1024], replicated, may hold values from 0.1 to 1.9
- first_bias: float32 [1024], replicated, may hold values from -2 to 2
- project_in: bfloat16 [1024, 3072], replicated, may hold values from -0.1875 to 0.1875
- project_out: bfloat16 [1024, 1024], replicated, may hold values from -2 to 2
- second_gain: float32 [1024], replicated, may hold values from 0.1 to 1.9
- second_bias: float32 [1024], replicated, may hold values from -2 to 2
- expert_in: bfloat16 [16, 1024, 4096], P('expert', None, 'hidden'), may hold values from -0.1875 to 0.1875
- expert_out: bfloat16 [16, 4096, 1024], P('expert', 'hidden'), may hold values from -0.09375 to 0.09375
- cotangent: bfloat16 [16384, 1024], P(('expert', 'hidden')), may hold values from -6 to 6
Outputs:
- block_out: bfloat16 [16384, 1024], P(('expert', 'hidden'))
- grad_tokens: float32 [16384, 1024], P(('expert', 'hidden'))
- grad_first_gain: float32 [1024], replicated
- grad_first_bias: float32 [1024], replicated
- grad_project_in: float32 [1024, 3072], replicated
- grad_project_out: float32 [1024, 1024], replicated
- grad_second_gain: float32 [1024], replicated
- grad_second_bias: float32 [1024], replicated
- grad_expert_in: float32 [16, 1024, 4096], P('expert', None, 'hidden')
- grad_expert_out: float32 [16, 4096, 1024], P('expert', 'hidden')
Inputs may be any that keep to these rules, and one draw needn't show every extreme that they name: Every token id v has hash_table[v] = its expert; each expert is named by 500 ids or one more. `token_ids`: among one device's 512 tokens at most 96 map to one expert through hash_table, and some expert gets exactly 96.
All inputs are finite; a program needn't handle non-finite values.
Results may differ from a plain program's by a relative error of at most 0.013.
Values may be sent and summed in bfloat16 or wider, within the bound.
A program may use at most 256 MiB of HBM per device.

v0:
```python
import jax
import jax.numpy as jnp
from jax import lax
from jax.sharding import PartitionSpec as P

HEADS = 16
HEAD_DIM = 64
SEQ = 512


def layer_norm(values, gain, bias):
    centered = values - jnp.mean(values, -1, keepdims=True)
    spread = jnp.mean(centered * centered, -1, keepdims=True)
    return centered * lax.rsqrt(spread + 1e-05) * gain + bias


def causal_scores(query, keys):
    length = query.shape[0]
    router_scores = jnp.einsum(
        "qhd,khd->hqk", query, keys, preferred_element_type=jnp.float32
    ) * query.shape[-1] ** (-0.5)
    earlier = lax.broadcasted_iota(jnp.int32, (length, length), 0)
    later = lax.broadcasted_iota(jnp.int32, (length, length), 1)
    return jnp.where(later <= earlier, router_scores, -1e30)


def on_device(
    tokens,
    token_ids,
    hash_table,
    first_gain,
    first_bias,
    project_in,
    project_out,
    second_gain,
    second_bias,
    expert_in,
    expert_out,
    cotangent,
):
    rows_dev, width = tokens.shape
    expert_devs = lax.axis_size("expert")
    local_experts = expert_in.shape[0]
    experts = local_experts * expert_devs
    capacity = 8 * ((3 * rows_dev + 8 * experts - 1) // (8 * experts))
    sequences = tokens.astype(jnp.float32).reshape(-1, SEQ, width)
    scale = HEAD_DIM ** (-0.5)

    def attend(inputs):
        normed = layer_norm(inputs, first_gain, first_bias).astype(jnp.bfloat16)
        merged = jnp.dot(normed, project_in, preferred_element_type=jnp.float32).astype(
            jnp.bfloat16
        )
        parts = merged.reshape(SEQ, 3, HEADS, HEAD_DIM)
        router_scores = causal_scores(parts[:, 0], parts[:, 1])
        top = jnp.max(router_scores, -1, keepdims=True)
        weights = jnp.exp(router_scores - top)
        total = jnp.sum(weights, -1, keepdims=True)
        shares_low = (weights / total).astype(jnp.bfloat16)
        attended = jnp.einsum(
            "hqk,khd->qhd", shares_low, parts[:, 2], preferred_element_type=jnp.float32
        )
        attended = attended.astype(jnp.bfloat16).reshape(SEQ, width)
        residual = inputs + jnp.dot(attended, project_out, preferred_element_type=jnp.float32)
        return (residual, merged, attended, top + jnp.log(total))

    residual, merged, attended, log_total = lax.map(attend, sequences)
    residual_flat = residual.reshape(rows_dev, width)
    second, pull_second = jax.vjp(layer_norm, residual_flat, second_gain, second_bias)
    sent = second.astype(jnp.bfloat16)
    owner = jnp.take(hash_table, token_ids)
    onehot = (owner[:, None] == jnp.arange(experts, dtype=jnp.int32)[None, :]).astype(jnp.int32)
    before_count = jnp.cumsum(onehot, 0, dtype=jnp.int32) - onehot
    place = owner * capacity + jnp.sum(before_count * onehot, 1, dtype=jnp.int32)

    def to_slots(values):
        slots = jnp.zeros((experts * capacity, width), jnp.bfloat16).at[place].set(values)
        return slots.reshape(expert_devs, local_experts, capacity, width)

    arrived = lax.all_to_all(
        to_slots(sent), "expert", split_axis=0, concat_axis=2, tiled=True
    ).reshape(local_experts, -1, width)
    gathered = lax.all_gather(arrived, "hidden", axis=1, tiled=True)
    before = jnp.einsum("erd,edf->erf", gathered, expert_in, preferred_element_type=jnp.float32)
    activated = jax.nn.gelu(before).astype(jnp.bfloat16)
    partial_out = jnp.einsum(
        "erf,efd->erd", activated, expert_out, preferred_element_type=jnp.float32
    )
    summed = lax.psum_scatter(
        partial_out.astype(jnp.bfloat16), "hidden", scatter_dimension=1, tiled=True
    )
    returned = lax.all_to_all(
        summed.reshape(1, local_experts, -1, width),
        "expert",
        split_axis=2,
        concat_axis=0,
        tiled=True,
    )
    returned = returned.reshape(experts * capacity, width)
    block_out = (residual_flat + returned[place].astype(jnp.float32)).astype(jnp.bfloat16)
    grad_arrived = lax.all_to_all(
        to_slots(cotangent), "expert", split_axis=0, concat_axis=2, tiled=True
    ).reshape(local_experts, -1, width)
    grad_members, members_back = (
        lax.all_gather(grad_arrived, "hidden", axis=1, tiled=True),
        lax.all_gather(arrived, "hidden", axis=1, tiled=True),
    )
    before_back = jnp.einsum(
        "erd,edf->erf", members_back, expert_in, preferred_element_type=jnp.float32
    )
    after_back, pull_gelu = jax.vjp(jax.nn.gelu, before_back)
    d_after = jnp.einsum(
        "erd,efd->erf", grad_members, expert_out, preferred_element_type=jnp.float32
    )
    d_before = pull_gelu(d_after)[0].astype(jnp.bfloat16)
    grad_expert_out = jnp.einsum(
        "erf,erd->efd",
        after_back.astype(jnp.bfloat16),
        grad_members,
        preferred_element_type=jnp.float32,
    )
    grad_expert_in = jnp.einsum(
        "erd,erf->edf", members_back, d_before, preferred_element_type=jnp.float32
    )
    d_members = jnp.einsum("erf,edf->erd", d_before, expert_in, preferred_element_type=jnp.float32)
    d_summed = lax.psum_scatter(
        d_members.astype(jnp.bfloat16), "hidden", scatter_dimension=1, tiled=True
    )
    d_returned = lax.all_to_all(
        d_summed.reshape(1, local_experts, -1, width),
        "expert",
        split_axis=2,
        concat_axis=0,
        tiled=True,
    )
    d_second = d_returned.reshape(experts * capacity, width)[place].astype(jnp.float32)
    d_residual, grad_second_gain, grad_second_bias = pull_second(d_second)
    d_residual = d_residual + cotangent.astype(jnp.float32)

    def attend_back(carry, inputs):
        grad_in, grad_out, grad_gain, grad_bias = carry
        source, merged_seq, attended_seq, log_seq, d_seq = inputs
        normed, pull_first = jax.vjp(layer_norm, source, first_gain, first_bias)
        d_branch = d_seq.astype(jnp.bfloat16)
        grad_out = grad_out + jnp.dot(attended_seq.T, d_branch, preferred_element_type=jnp.float32)
        d_attended = jnp.dot(d_branch, project_out.T, preferred_element_type=jnp.float32)
        d_attended = d_attended.astype(jnp.bfloat16).reshape(SEQ, HEADS, HEAD_DIM)
        parts = merged_seq.reshape(SEQ, 3, HEADS, HEAD_DIM)
        query, keys, values = (parts[:, 0], parts[:, 1], parts[:, 2])
        shares = jnp.exp(causal_scores(query, keys) - log_seq)
        d_shares = jnp.einsum(
            "qhd,khd->hqk", d_attended, values, preferred_element_type=jnp.float32
        )
        d_scores = (shares * (d_shares - jnp.sum(shares * d_shares, -1, keepdims=True))).astype(
            jnp.bfloat16
        )
        d_query = (
            jnp.einsum("hqk,khd->qhd", d_scores, keys, preferred_element_type=jnp.float32) * scale
        )
        d_keys = (
            jnp.einsum("hqk,qhd->khd", d_scores, query, preferred_element_type=jnp.float32) * scale
        )
        d_values = jnp.einsum(
            "hqk,qhd->khd",
            shares.astype(jnp.bfloat16),
            d_attended,
            preferred_element_type=jnp.float32,
        )
        d_merged = (
            jnp.stack([d_query, d_keys, d_values], 1).reshape(SEQ, 3 * width).astype(jnp.bfloat16)
        )
        grad_in = grad_in + jnp.dot(
            normed.astype(jnp.bfloat16).T, d_merged, preferred_element_type=jnp.float32
        )
        d_normed = jnp.dot(d_merged, project_in.T, preferred_element_type=jnp.float32)
        d_source, d_gain, d_bias = pull_first(d_normed)
        return ((grad_in, grad_out, grad_gain + d_gain, grad_bias + d_bias), d_seq + d_source)

    start = (
        jnp.zeros((width, 3 * width), jnp.float32),
        jnp.zeros((width, width), jnp.float32),
        jnp.zeros((width,), jnp.float32),
        jnp.zeros((width,), jnp.float32),
    )
    carry, grad_tokens = lax.scan(
        attend_back,
        start,
        (sequences, merged, attended, log_total, d_residual.reshape(-1, SEQ, width)),
    )
    grad_in, grad_out, grad_first_gain, grad_first_bias = carry
    grad_in, grad_out, grad_first_gain, grad_first_bias, grad_second_gain, grad_second_bias = (
        lax.psum(
            (
                grad_in,
                grad_out,
                grad_first_gain,
                grad_first_bias,
                grad_second_gain,
                grad_second_bias,
            ),
            ("expert", "hidden"),
        )
    )
    return (
        block_out,
        grad_tokens.reshape(rows_dev, width),
        grad_first_gain,
        grad_first_bias,
        grad_in,
        grad_out,
        grad_second_gain,
        grad_second_bias,
        grad_expert_in,
        grad_expert_out,
    )


def solution(mesh):
    placed = (
        P(("expert", "hidden"), None),
        P(("expert", "hidden")),
        P(),
        P(),
        P(),
        P(),
        P(),
        P(),
        P(),
        P("expert", None, "hidden"),
        P("expert", "hidden", None),
        P(("expert", "hidden"), None),
    )
    return jax.shard_map(
        on_device,
        mesh=mesh,
        in_specs=placed,
        out_specs=(
            P(("expert", "hidden"), None),
            P(("expert", "hidden"), None),
            P(),
            P(),
            P(),
            P(),
            P(),
            P(),
            P("expert", None, "hidden"),
            P("expert", "hidden", None),
        ),
        check_vma=False,
    )
```

profile of v0, /device:TPU:0, one launch (start us, length us, event | category | flops | bytes accessed | tf_op | source)
XLA Modules:
  0.0 1398.7 jit_solution(8726764986137051140)
XLA Ops:
  8.1 3.4 gather_fusion
  13.7 5.4 scatter_custom_fusion.1
  19.1 43.0 %all_to_all.60 = bf16[8,2,96,1024]{3,2,1,0:T(8,128)(2,1)S(1)} all-to-all(bf16[8,2,96,1024]{3,2,1,0:T(8,128)(2,1)} %bitcast.114), channel_id=1, replica_groups=mesh['expert'=8,'hidden'=4] {'expert'}, dimensions={0} | all-to-all | bytes 6291456 | tf_op jit(solution)/shard_map/all_to_all | solution.py:101
  62.1 2.1 copy.54
  67.3 7.8 convolution_convert_fusion.2
  75.1 5.0 copy.48
  80.1 9.9 fusion.60
  90.1 8.3 fusion.7
  98.4 9.2 fusion.32
  110.7 6.2 scatter_custom_fusion
  116.9 41.4 %all_to_all.61 = bf16[8,2,96,1024]{3,2,1,0:T(8,128)(2,1)S(1)} all-to-all(bf16[8,2,96,1024]{3,2,1,0:T(8,128)(2,1)} %bitcast.112), channel_id=1, replica_groups=mesh['expert'=8,'hidden'=4] {'expert'}, dimensions={0} | all-to-all | bytes 6291456 | tf_op jit(solution)/shard_map/all_to_all | solution.py:80
  158.3 2.1 copy.51
  160.5 121.5 %all-gather.5.cloned.1.call-done = bf16[2,3072,1024]{2,1,0:T(8,128)(2,1)} async-done(((bf16[2,768,1024]{2,1,0:T(8,128)(2,1)}), bf16[2,3072,1024]{2,1,0:T(8,128)(2,1)}) %all-gather.5.cloned.1.call-update) | async-done | bytes 12582928 | tf_op jit(solution)/shard_map/all_gather | solution.py:105
  282.0 22.1 %fusion.62 = f32[2,3072,1024]{2,1,0:T(8,128)} fusion(bf16[2,3072,1024]{2,1,0:T(8,128)(2,1)} %all-gather.5.cloned.1.call-done, bf16[2,1024,1024]{2,1,0:T(8,128)(2,1)} %param.22), kind=kOutput, calls=%fused_computation.112 | convolution fusion | flops 12884901888 | bytes 41943040 | tf_op jit(solution)/shard_map/erd,efd->erf/dot_general | solution.py:112
  304.0 196.5 %all-gather.3.cloned.1.call-done = bf16[2,3072,1024]{2,1,0:T(8,128)(2,1)} async-done(((bf16[2,768,1024]{2,1,0:T(8,128)(2,1)}), bf16[2,3072,1024]{2,1,0:T(8,128)(2,1)}) %all-gather.3.cloned.1.call-update) | async-done | bytes 12582928 | tf_op jit(solution)/shard_map/all_gather | solution.py:83
  500.5 37.7 %fusion.6 = (bf16[2,3072,1024]{2,1,0:T(8,128)(2,1)}, f32[2,3072,1024]{2,1,0:T(8,128)}) fusion(f32[2,3072,1024]{2,1,0:T(8,128)} %fusion.62, bf16[2,3072,1024]{2,1,0:T(8,128)(2,1)} %all-gather.3.cloned.1.call-done, bf16[2,1024,1024]{2,1,0:T(8,128)(2,1)} %param.21), kind=kOutput, calls=%fused_computation.13 | convolution fusion | flops 13010731008 | bytes 79691776 | tf_op jit(solution)/shard_map/erd,edf->erf/dot_general | solution.py:84
  538.3 20.6 %convolution_convert_fusion = bf16[2,3072,1024]{2,1,0:T(8,128)(2,1)} fusion(bf16[2,3072,1024]{2,1,0:T(8,128)(2,1)} %get-tuple-element.105, bf16[2,1024,1024]{2,1,0:T(8,128)(2,1)} %param.21), kind=kOutput, calls=%fused_computation.26 | convolution fusion | flops 12891193344 | bytes 29360128 | tf_op jit(solution)/shard_map/erf,edf->erd/dot_general | solution.py:125
  558.9 25.8 %convolution_convert_fusion.1 = bf16[2,3072,1024]{2,1,0:T(8,128)(2,1)} fusion(bf16[2,1024,1024]{2,1,0:T(8,128)(2,1)} %param.22, f32[2,3072,1024]{2,1,0:T(8,128)} %get-tuple-element.106), kind=kOutput, calls=%fused_computation.27 | convolution fusion | flops 12947816448 | bytes 41943040 | tf_op jit(solution)/shard_map/erf,efd->erd/dot_general | solution.py:86
  584.8 184.3 %reduce-scatter.5.cloned.1.call-done = bf16[2,768,1024]{2,1,0:T(8,128)(2,1)} async-done(((bf16[2,3072,1024]{2,1,0:T(8,128)(2,1)}), bf16[2,768,1024]{2,1,0:T(8,128)(2,1)}) %reduce-scatter.5.cloned.1.call-update) | async-done | bytes 3145744 | tf_op jit(solution)/shard_map/reduce_scatter | solution.py:126
  769.1 6.8 copy.55
  775.9 5.0 all-to-all-start.3
  780.9 203.4 %reduce-scatter.3.cloned.1.call-done = bf16[2,768,1024]{2,1,0:T(8,128)(2,1)} async-done(((bf16[2,3072,1024]{2,1,0:T(8,128)(2,1)}), bf16[2,768,1024]{2,1,0:T(8,128)(2,1)}) %reduce-scatter.3.cloned.1.call-update) | async-done | bytes 3145744 | tf_op jit(solution)/shard_map/reduce_scatter | solution.py:89
  984.2 6.8 copy.52
  991.0 4.6 all-to-all-start.1
  995.8 4.6 copy.56
  1000.3 5.1 gather_fusion.2
  1005.5 2.4 fusion.27
  1007.9 25.7 %all-to-all-done.1 = bf16[1,2,768,1024]{3,1,0,2:T(2,128)(2,1)} async-done(((bf16[1,2,768,1024]{3,1,0,2:T(2,128)(2,1)}), bf16[1,2,768,1024]{3,1,0,2:T(2,128)(2,1)}, u32[]{:S(2)}, u32[]{:S(2)}) %all-to-all-start.1) | async-done | bytes 3145760 | tf_op jit(solution)/shard_map/all_to_all | solution.py:92
  1033.6 4.5 copy.53
  1038.1 5.8 gather_fusion.1
  1043.9 3.8 fusion.59
  1048.0 2.3 convolution_convert_fusion.3
  1050.3 3.3 fusion.63
  1053.5 1.5 copy.57
  1055.0 8.6 fusion.38
  1063.6 10.8 multiply_reduce_fusion
  1074.4 11.8 multiply_convert_fusion.1
  1086.2 2.6 fusion.37
  1090.8 1.6 copy-done.9
  1092.4 6.9 fusion.53
  1099.4 20.1 %fusion.64 = f32[2,1024,1024]{2,1,0:T(8,128)} fusion(bf16[2,3072,1024]{2,1,0:T(8,128)(2,1)} %all-gather.3.cloned.1.call-done, bf16[2,3072,1024]{2,1,0:T(8,128)(2,1)} %get-tuple-element.105), kind=kOutput, calls=%fused_computation.114 | convolution fusion | flops 12884901888 | bytes 33554432 | tf_op jit(solution)/shard_map/erd,erf->edf/dot_general | solution.py:122
  1119.5 24.6 %fusion.57 = f32[2,1024,1024]{2,1,0:T(8,128)} fusion(bf16[2,3072,1024]{2,1,0:T(8,128)(2,1)} %all-gather.5.cloned.1.call-done, f32[2,3072,1024]{2,1,0:T(8,128)} %get-tuple-element.106), kind=kOutput, calls=%fused_computation.107 | convolution fusion | flops 12941524992 | bytes 46137344 | tf_op jit(solution)/shard_map/erf,erd->efd/dot_general | solution.py:116
  1144.1 7.4 fusion.58
  1153.9 42.6 %all-reduce = (f32[1024]{0:T(1024)}, f32[1024]{0:T(1024)}, f32[1024]{0:T(1024)}, f32[1024]{0:T(1024)}) all-reduce(f32[1024]{0:T(1024)S(1)} %get-tuple-element.70, f32[1024]{0:T(1024)S(1)} %get-tuple-element.74, f32[1024]{0:T(1024)S(1)} %get-tuple-element.72, ...), channel_id=1, replica_groups=mesh['expert'=8,'hidden'=4] {'expert','hidden'}, use_global_device_ids=true, to_apply=%region_19.20 | all-reduce | flops 4096 | bytes 32768 | tf_op jit(solution)/shard_map/psum | solution.py:192
  1196.5 4.7 add_add_fusion.2
  1201.3 177.5 %all-reduce.4.cloned.1.call-done = (f32[1024,3072]{1,0:T(8,128)}, f32[1024,1024]{1,0:T(8,128)}) async-done(((f32[1024,3072]{1,0:T(8,128)}, f32[1024,1024]{1,0:T(8,128)}), (f32[1024,3072]{1,0:T(8,128)}, f32[1024,1024]{1,0:T(8,128)})) %all-reduce.4.cloned.1.call-update) | async-done | bytes 16777232 | tf_op jit(solution)/shard_map/psum | solution.py:192
  1378.8 11.1 copy.73
  1389.9 2.0 copy.74
  (113 shorter events, 14.1 us)
Async XLA Ops:
  7.2 100.4 %copy-start = (bf16[1024,1024]{1,0:T(8,128)(2,1)S(1)}, bf16[1024,1024]{1,0:T(8,128)(2,1)}, u32[]{:S(2)}) copy-start(bf16[1024,1024]{1,0:T(8,128)(2,1)} %param.18) | copy-start | bytes 6291460
  7.2 274.8 %all-gather.5.cloned.1.call-start = ((), (), s32[]{:S(2)}) async-start(), calls=%async_computation.8 | async-start | bytes 15728640 | tf_op jit(solution)/shard_map/all_gather | solution.py:105
  13.7 97.0 %copy-start.32 = (s32[512]{0:T(512)}, s32[512]{0:T(512)S(1)}, u32[]{:S(2)}) copy-start(s32[512]{0:T(512)S(1)} %compare_select_fusion) | copy-start | bytes 6148
  64.2 1.2 copy-start.3
  64.2 3.1 copy-start.30
  64.2 3.1 copy-start.35
  64.2 436.3 %all-gather.3.cloned.1.call-start = ((), (), s32[]{:S(2)}) async-start(), calls=%async_computation.6 | async-start | bytes 15728640 | tf_op jit(solution)/shard_map/all_gather | solution.py:83
  65.6 1.0 copy-start.20
  66.1 0.6 copy-start.26
  66.7 0.6 copy-start.24
  90.0 8.3 copy-start.12
  98.4 9.2 copy-start.14
  107.6 1.4 copy-start.10
  107.6 3.1 copy-start.18
  107.6 3.1 copy-start.34
  109.0 1.3 copy-start.1
  109.0 7.9 copy-start.16
  110.7 47.7 %copy-start.28 = (f32[512]{0:T(512)}, f32[512]{0:T(512)S(1)}, u32[]{:S(2)}) copy-start(f32[512]{0:T(512)S(1)} %multiply_reduce_fusion.1) | copy-start | bytes 6148
  110.7 47.6 %copy-start.22 = (f32[512]{0:T(512)}, f32[512]{0:T(512)S(1)}, u32[]{:S(2)}) copy-start(f32[512]{0:T(512)S(1)} %fusion.52) | copy-start | bytes 6148
  160.4 608.7 %reduce-scatter.5.cloned.1.call-start = ((), (), s32[]{:S(2)}) async-start(), calls=%async_computation.9 | async-start | bytes 15728640 | tf_op jit(solution)/shard_map/reduce_scatter | solution.py:126
  558.9 425.4 %reduce-scatter.3.cloned.1.call-start = ((), (), s32[]{:S(2)}) async-start(), calls=%async_computation.7 | async-start | bytes 15728640 | tf_op jit(solution)/shard_map/reduce_scatter | solution.py:89
  775.9 215.2 %all-to-all-start.3 = ((bf16[1,2,768,1024]{3,1,0,2:T(2,128)(2,1)}), bf16[1,2,768,1024]{3,1,0,2:T(2,128)(2,1)}, u32[]{:S(2)}, u32[]{:S(2)}) async-start(bf16[1,2,768,1024]{3,1,0,2:T(2,128)(2,1)} %copy.55), calls=%async_computation.5 | async-start | bytes 6291456 | tf_op jit(solution)/shard_map/all_to_all | solution.py:129
  991.0 4.7 copy-start.33
  991.0 4.7 copy-start.13
  991.0 4.7 copy-start.15
  991.0 42.5 %all-to-all-start.1 = ((bf16[1,2,768,1024]{3,1,0,2:T(2,128)(2,1)}), bf16[1,2,768,1024]{3,1,0,2:T(2,128)(2,1)}, u32[]{:S(2)}, u32[]{:S(2)}) async-start(bf16[1,2,768,1024]{3,1,0,2:T(2,128)(2,1)} %copy.52), calls=%async_computation.2 | async-start | bytes 6291456 | tf_op jit(solution)/shard_map/all_to_all | solution.py:92
  995.7 383.1 %all-reduce.4.cloned.1.call-start = ((), (), s32[]{:S(2)}) async-start(), calls=%async_computation.10 | async-start | bytes 33554432 | tf_op jit(solution)/shard_map/psum | solution.py:192
  1000.3 5.1 copy-start.17
  1000.3 5.1 copy-start.19
  1000.3 5.1 copy-start.23
  1005.4 2.4 copy-start.29
  1043.9 3.8 copy-start.8
  1047.6 2.6 copy-start.5
  1048.0 2.3 copy-start.11
  1055.0 8.6 copy-start.2
  1090.4 2.0 copy-start.4
  1090.4 2.0 copy-start.21
  1090.4 2.0 copy-start.25
  1090.4 2.0 copy-start.31
  1090.4 2.0 copy-start.36
  1090.8 1.6 copy-start.9
  1144.1 7.5 copy-start.27
  1151.6 1.3 copy-start.6
  1378.8 11.1 copy-start.7
Sparse Core Ops, SparseCore 0:
  64.4 217.5 all-gather.4
  284.1 216.3 all-gather.2
  559.0 210.0 reduce-scatter.4
  771.3 212.8 reduce-scatter.2
  1099.5 279.2 all-reduce.3
where the time goes:
time: 1410 us; the launch traced here: 1400 us
  waiting for transfers between devices  909 us (64%)
  matrix products  223 us (16%)
  blocking collectives  127 us (9%)
  local copies, waits for them, and re-layouts  73 us (5%)
  other arithmetic  42.9 us (3%)
  between operations  14.5 us (1%)
    reduce_scatter x1, waiting for transfers between devices, on_device(): lax.psum_scatter(partial_out.astype(jnp.bfloat16), 'hidden', scatter_dime...  203 us
    all_gather x1, waiting for transfers between devices, on_device(): gathered = lax.all_gather(arrived, 'hidden', axis=1, tiled=True)  196 us
    reduce_scatter x1, waiting for transfers between devices, on_device(): lax.psum_scatter(d_members.astype(jnp.bfloat16), 'hidden', scatter_dimens...  184 us
    psum x1, waiting for transfers between devices, on_device(): lax.psum((grad_in, grad_out, grad_first_gain, grad_first_bias, grad_secon...  177 us
    all_gather x1, waiting for transfers between devices, on_device(): lax.all_gather(grad_arrived, 'hidden', axis=1, tiled=True)  121 us
    all_to_all x1, blocking collectives, on_device(): lax.all_to_all(to_slots(cotangent), 'expert', split_axis=0, concat_axis=2...  43 us
    psum x1, blocking collectives, on_device(): lax.psum((grad_in, grad_out, grad_first_gain, grad_first_bias, grad_secon...  42.6 us
    all_to_all x1, blocking collectives, on_device(): lax.all_to_all(to_slots(sent), 'expert', split_axis=0, concat_axis=2, til...  41.4 us
  transfers between devices with their start and end apart: 7, of which 6 were waited for; matrix products, arithmetic and copies ran while one was open for 13% of the time, Pallas kernels for 0%

commit v1 on v0

v1 whole, which is shorter than its diff:
```python
import functools

import jax
import jax.numpy as jnp
from jax import lax
from jax.experimental import pallas as pl
from jax.experimental.pallas import tpu as pltpu
from jax.sharding import PartitionSpec as P

HEADS = 16
HEAD_DIM = 64
SEQ = 512
TILE = 256
EPS = 1e-05
BF = jnp.bfloat16
F32 = jnp.float32


def layer_norm(values, gain, bias):
    centered = values - jnp.mean(values, -1, keepdims=True)
    spread = jnp.mean(centered * centered, -1, keepdims=True)
    return centered * lax.rsqrt(spread + EPS) * gain + bias


def causal_scores(query, keys):
    length = query.shape[0]
    scores = jnp.einsum(
        "qhd,khd->hqk", query, keys, preferred_element_type=F32
    ) * query.shape[-1] ** (-0.5)
    earlier = lax.broadcasted_iota(jnp.int32, (length, length), 0)
    later = lax.broadcasted_iota(jnp.int32, (length, length), 1)
    return jnp.where(later <= earlier, scores, -1e30)


def dot(a, b, dims=((1,), (0,))):
    return lax.dot_general(a, b, (dims, ((), ())), preferred_element_type=F32)


def expert_kernel(local_experts, has, x, cot, eid, w_in, w_out, act_o, dbef_o, part_o, dmem_o):
    tile = pl.program_id(0)
    outs = (act_o, dbef_o, part_o, dmem_o)

    @pl.when(has[tile, 0] == 0)
    def _():
        for out in outs:
            out[...] = jnp.zeros(out.shape, out.dtype)

    for expert in range(local_experts):

        @pl.when(has[tile, expert] > 0)
        def _(expert=expert):
            mine = eid[...] == float(expert)
            before = dot(x[...], w_in[expert])
            d_after = dot(cot[...], w_out[expert], ((1,), (1,)))
            square = before * before
            inner = 0.7978845608028654 * before * (1.0 + 0.044715 * square)
            tanh = jnp.tanh(inner)
            half = 0.5 * (1.0 + tanh)
            act = (before * half).astype(BF)
            slope = half + 0.5 * before * (1.0 - tanh * tanh) * (
                0.7978845608028654 * (1.0 + 0.134145 * square)
            )
            dbef = (d_after * slope).astype(BF)
            part = dot(act, w_out[expert])
            dmem = dot(dbef, w_in[expert], ((1,), (1,)))
            news = (act.astype(F32), dbef.astype(F32), part, dmem)
            for out, new in zip(outs, news):
                old = 0.0 if expert == 0 else out[...].astype(F32)
                out[...] = jnp.where(mine, new, old).astype(BF)


def expert_rows(x, cot, eid, has, w_in, w_out):
    rows, width = x.shape
    experts, _, hidden = w_in.shape
    tiles = rows // TILE
    row_block = pl.BlockSpec((TILE, width), lambda t, has: (t, 0))
    hid_block = pl.BlockSpec((TILE, hidden), lambda t, has: (t, 0))
    whole = lambda shape: pl.BlockSpec(shape, lambda t, has: (0, 0, 0), pipeline_mode=pl.Buffered(1))
    return pl.pallas_call(
        functools.partial(expert_kernel, experts),
        grid_spec=pltpu.PrefetchScalarGridSpec(
            num_scalar_prefetch=1,
            grid=(tiles,),
            in_specs=[
                row_block,
                row_block,
                pl.BlockSpec((TILE, 1), lambda t, has: (t, 0)),
                whole(w_in.shape),
                whole(w_out.shape),
            ],
            out_specs=[hid_block, hid_block, row_block, row_block],
        ),
        out_shape=[
            jax.ShapeDtypeStruct((rows, hidden), BF),
            jax.ShapeDtypeStruct((rows, hidden), BF),
            jax.ShapeDtypeStruct((rows, width), BF),
            jax.ShapeDtypeStruct((rows, width), BF),
        ],
        compiler_params=pltpu.CompilerParams(vmem_limit_bytes=56 * 2**20),
        cost_estimate=pl.CostEstimate(
            flops=8 * rows * width * hidden,
            bytes_accessed=2 * (w_in.size + w_out.size + 6 * rows * width),
            transcendentals=rows * hidden,
        ),
        name="expert_rows",
    )(has, x, cot, eid, w_in, w_out)


def expert_grad_kernel(has, x, cot, eid, act, dbef, g_in, g_out):
    expert, tile = pl.program_id(0), pl.program_id(1)

    @pl.when(tile == 0)
    def _():
        g_in[...] = jnp.zeros(g_in.shape, F32)
        g_out[...] = jnp.zeros(g_out.shape, F32)

    @pl.when(has[tile, expert] > 0)
    def _():
        mine = jnp.where(eid[...] == expert.astype(F32), 1.0, 0.0).astype(BF)
        g_in[0] += dot(x[...], dbef[...] * mine, ((0,), (0,)))
        g_out[0] += dot(act[...] * mine, cot[...], ((0,), (0,)))


def expert_grads(x, cot, eid, has, act, dbef):
    rows, width = x.shape
    hidden = act.shape[1]
    tiles, experts = has.shape
    row_block = pl.BlockSpec((TILE, width), lambda e, t, has: (t, 0))
    hid_block = pl.BlockSpec((TILE, hidden), lambda e, t, has: (t, 0))
    return pl.pallas_call(
        expert_grad_kernel,
        grid_spec=pltpu.PrefetchScalarGridSpec(
            num_scalar_prefetch=1,
            grid=(experts, tiles),
            in_specs=[
                row_block,
                row_block,
                pl.BlockSpec((TILE, 1), lambda e, t, has: (t, 0)),
                hid_block,
                hid_block,
            ],
            out_specs=[
                pl.BlockSpec((1, width, hidden), lambda e, t, has: (e, 0, 0)),
                pl.BlockSpec((1, hidden, width), lambda e, t, has: (e, 0, 0)),
            ],
        ),
        out_shape=[
            jax.ShapeDtypeStruct((experts, width, hidden), F32),
            jax.ShapeDtypeStruct((experts, hidden, width), F32),
        ],
        compiler_params=pltpu.CompilerParams(vmem_limit_bytes=56 * 2**20),
        cost_estimate=pl.CostEstimate(
            flops=4 * rows * width * hidden,
            bytes_accessed=8 * experts * width * hidden + 16 * rows * width,
            transcendentals=0,
        ),
        name="expert_grads",
    )(has, x, cot, eid, act, dbef)


def on_device(
    tokens,
    token_ids,
    hash_table,
    first_gain,
    first_bias,
    project_in,
    project_out,
    second_gain,
    second_bias,
    expert_in,
    expert_out,
    cotangent,
):
    rows_dev, width = tokens.shape
    expert_devs = lax.axis_size("expert")
    hidden_devs = lax.axis_size("hidden")
    local = expert_in.shape[0]
    experts = local * expert_devs
    capacity = 8 * ((3 * rows_dev + 8 * experts - 1) // (8 * experts))
    chunk = local * capacity
    scale = HEAD_DIM ** (-0.5)

    owner = hash_table.at[token_ids].get(mode="promise_in_bounds")
    expert_ids = jnp.arange(experts, dtype=jnp.int32)
    onehot = owner[:, None] == expert_ids[None, :]
    earlier = lax.broadcasted_iota(jnp.int32, (rows_dev, rows_dev), 1) < lax.broadcasted_iota(
        jnp.int32, (rows_dev, rows_dev), 0
    )
    before_count = jnp.dot(earlier.astype(BF), onehot.astype(BF), preferred_element_type=F32)
    counts = jnp.sum(onehot.astype(jnp.int32), 0)
    grouped = counts.reshape(expert_devs, local)
    first_slot = (
        jnp.cumsum(grouped, 1) - grouped + jnp.arange(expert_devs, dtype=jnp.int32)[:, None] * chunk
    ).reshape(experts)
    place = jnp.sum(
        jnp.where(onehot, before_count.astype(jnp.int32) + first_slot[None, :], 0), 1
    )
    all_counts = lax.all_gather(counts, ("expert", "hidden")).reshape(
        expert_devs, hidden_devs, expert_devs, local
    )
    group = lax.axis_index("expert")
    plane = lax.axis_index("hidden")
    group_counts = lax.dynamic_index_in_dim(all_counts, group, 2, keepdims=False)
    most = jnp.max(jnp.sum(all_counts, (0, 3)))

    def run(rows):
        send = (
            place[None, :] == jnp.arange(expert_devs * chunk, dtype=jnp.int32)[:, None]
        ).astype(BF)

        mine = lax.dynamic_index_in_dim(group_counts, plane, 1, keepdims=False)
        starts = jnp.cumsum(mine, 1) - mine
        totals = jnp.sum(mine, 0)
        bases = jnp.cumsum(mine, 0) - mine + (jnp.cumsum(totals) - totals)[None, :]
        slot = jnp.arange(chunk, dtype=jnp.int32)[None, :]
        target = jnp.full((expert_devs, chunk), -1, jnp.int32)
        for l in range(local):
            offset = slot - starts[:, l : l + 1]
            target = jnp.where(
                (offset >= 0) & (offset < mine[:, l : l + 1]), bases[:, l : l + 1] + offset, target
            )
        target = target.reshape(-1)
        pack = (target[None, :] == jnp.arange(rows, dtype=jnp.int32)[:, None]).astype(BF)
        plane_totals = jnp.sum(group_counts, 0)
        ends = jnp.cumsum(plane_totals, 1)
        row = jnp.arange(rows, dtype=jnp.int32)[None, :]
        eid = jnp.zeros((hidden_devs, rows), jnp.int32)
        for l in range(local):
            eid = eid + (row >= ends[:, l : l + 1]).astype(jnp.int32)
        eid = eid.reshape(-1, 1)
        has = jnp.stack(
            [jnp.any((eid == l).reshape(-1, TILE), 1).astype(jnp.int32) for l in range(local)], 1
        )
        eid = eid.astype(F32)

        def dispatch(values):
            slots = jnp.dot(send, values, preferred_element_type=F32).astype(BF)
            arrived = lax.all_to_all(
                slots.reshape(expert_devs, chunk, width), "expert", 0, 0, tiled=True
            )
            packed = jnp.dot(
                pack, arrived.reshape(-1, width), preferred_element_type=F32
            ).astype(BF)
            return lax.all_gather(packed, "hidden", axis=0, tiled=True)

        def give_back(partial):
            summed = lax.psum_scatter(partial, "hidden", scatter_dimension=0, tiled=True)
            slots = dot(pack, summed, ((0,), (0,))).astype(BF)
            returned = lax.all_to_all(
                slots.reshape(expert_devs, chunk, width), "expert", 0, 0, tiled=True
            )
            return dot(send, returned.reshape(-1, width), ((0,), (0,)))

        cot_rows = dispatch(cotangent)

        def attend(inputs):
            normed = layer_norm(inputs, first_gain, first_bias).astype(BF)
            merged = jnp.dot(normed, project_in, preferred_element_type=F32).astype(BF)
            parts = merged.reshape(SEQ, 3, HEADS, HEAD_DIM)
            scores = causal_scores(parts[:, 0], parts[:, 1])
            top = jnp.max(scores, -1, keepdims=True)
            weights = jnp.exp(scores - top)
            total = jnp.sum(weights, -1, keepdims=True)
            shares_low = (weights / total).astype(BF)
            attended = jnp.einsum(
                "hqk,khd->qhd", shares_low, parts[:, 2], preferred_element_type=F32
            )
            attended = attended.astype(BF).reshape(SEQ, width)
            residual = inputs + jnp.dot(attended, project_out, preferred_element_type=F32)
            return (residual, merged, attended, top + jnp.log(total))

        source = tokens.astype(F32)
        residual, merged, attended, log_total = attend(source)
        second, pull_second = jax.vjp(layer_norm, residual, second_gain, second_bias)
        x_rows = dispatch(second.astype(BF))
        act, dbef, part, dmem = expert_rows(x_rows, cot_rows, eid, has, expert_in, expert_out)
        d_second = give_back(dmem)
        produced = give_back(part)
        grad_expert_in, grad_expert_out = expert_grads(x_rows, cot_rows, eid, has, act, dbef)
        block_out = (residual + produced).astype(BF)
        d_residual, grad_second_gain, grad_second_bias = pull_second(d_second)
        d_residual = d_residual + cotangent.astype(F32)

        normed, pull_first = jax.vjp(layer_norm, source, first_gain, first_bias)
        d_branch = d_residual.astype(BF)
        grad_out = dot(attended, d_branch, ((0,), (0,)))
        d_attended = dot(d_branch, project_out, ((1,), (1,)))
        d_attended = d_attended.astype(BF).reshape(SEQ, HEADS, HEAD_DIM)
        parts = merged.reshape(SEQ, 3, HEADS, HEAD_DIM)
        query, keys, values = (parts[:, 0], parts[:, 1], parts[:, 2])
        shares = jnp.exp(causal_scores(query, keys) - log_total)
        d_shares = jnp.einsum("qhd,khd->hqk", d_attended, values, preferred_element_type=F32)
        d_scores = (shares * (d_shares - jnp.sum(shares * d_shares, -1, keepdims=True))).astype(BF)
        d_query = jnp.einsum("hqk,khd->qhd", d_scores, keys, preferred_element_type=F32) * scale
        d_keys = jnp.einsum("hqk,qhd->khd", d_scores, query, preferred_element_type=F32) * scale
        d_values = jnp.einsum(
            "hqk,qhd->khd", shares.astype(BF), d_attended, preferred_element_type=F32
        )
        d_merged = (
            jnp.stack([d_query, d_keys, d_values], 1).reshape(SEQ, 3 * width).astype(BF)
        )
        grad_in = dot(normed.astype(BF), d_merged, ((0,), (0,)))
        d_normed = dot(d_merged, project_in, ((1,), (1,)))
        d_source, grad_first_gain, grad_first_bias = pull_first(d_normed)
        small = jnp.stack([grad_first_gain, grad_first_bias, grad_second_gain, grad_second_bias])
        high = small.astype(BF)
        flat = jnp.concatenate(
            [
                grad_in.astype(BF).reshape(-1, width),
                grad_out.astype(BF),
                high,
                (small - high.astype(F32)).astype(BF),
            ]
        )
        flat = lax.psum(flat, ("expert", "hidden"))
        first = 3 * width
        second_end = first + width
        grad_in = flat[:first].astype(F32).reshape(width, 3 * width)
        grad_out = flat[first:second_end].astype(F32)
        small = flat[second_end : second_end + 4].astype(F32) + flat[second_end + 4 :].astype(F32)
        return (
            block_out,
            d_residual + d_source,
            small[0],
            small[1],
            grad_in,
            grad_out,
            small[2],
            small[3],
            grad_expert_in,
            grad_expert_out,
        )

    sizes = [size for size in (768, 896) if size < expert_devs * chunk] + [expert_devs * chunk]
    pick = sum((most > size).astype(jnp.int32) for size in sizes[:-1])
    return lax.switch(pick, [functools.partial(run, size) for size in sizes])


def solution(mesh):
    rows = P(("expert", "hidden"), None)
    w_in, w_out = P("expert", None, "hidden"), P("expert", "hidden", None)
    return jax.shard_map(
        on_device,
        mesh=mesh,
        in_specs=(
            rows,
            P(("expert", "hidden")),
            P(),
            P(),
            P(),
            P(),
            P(),
            P(),
            P(),
            w_in,
            w_out,
            rows,
        ),
        out_specs=(rows, rows, P(), P(), P(), P(), P(), P(), w_in, w_out),
        check_vma=False,
    )
```

time: 1410 us -> 914 us (0.65)
  waiting for transfers between devices: 909 us -> 455 us
  matrix products: 223 us -> 110 us
  Pallas kernels: 0 us -> 89.4 us
  blocking collectives: 127 us -> 82.5 us
    reduce_scatter x2, waiting for transfers between devices: 388 us -> 110 us  [give_back(): lax.psum_scatter(partial, 'hidden', scatter_dimension=0, tiled=True)]
    all_gather x2, waiting for transfers between devices: 318 us -> 137 us  [dispatch(): return lax.all_gather(packed, 'hidden', axis=0, tiled=True)]
    dot_general x17 -> x20, matrix products: 213 us -> 101 us  [the longest x8 35.8 us: dot(): return lax.dot_general(a, b, (dims, ((), ())), preferred_element_type=F32)]
    pallas_call x0 -> x2, Pallas kernels: none -> 89.4 us  [the longest x1 46.3 us: expert_rows(): pl.pallas_call(functools.partial(expert_kernel, experts), grid_spec=pltpu...]
    all_to_all x2 -> x3, waiting for transfers between devices: 25.7 us -> 76.4 us  [the longest x2 40.2 us: give_back(): lax.all_to_all(slots.reshape(expert_devs, chunk, width), 'expert', 0, 0,...]
    psum x1, waiting for transfers between devices: 177 us -> 131 us  [run(): flat = lax.psum(flat, ('expert', 'hidden'))]
    all_to_all x2 -> x1, blocking collectives: 84.4 us -> 40.5 us  [dispatch(): lax.all_to_all(slots.reshape(expert_devs, chunk, width), 'expert', 0, 0,...]
    psum x1 -> x0, blocking collectives: 42.6 us -> none  [on_device(): lax.psum((grad_in, grad_out, grad_first_gain, grad_first_bias, grad_secon...]
  transfers between devices with their start and end apart: 7 -> 8, of which waited for: 6 -> 7; matrix products, arithmetic and copies ran while one was open for 13% -> 20% of each run, Pallas kernels for 0% -> 5%
where the time goes in v1:
time: 914 us; the launch traced here: 906 us
  waiting for transfers between devices  455 us (50%)
  matrix products  110 us (12%)
  Pallas kernels  89.4 us (10%)
  local copies, waits for them, and re-layouts  85.8 us (9%)
  blocking collectives  82.5 us (9%)
  other arithmetic  42.9 us (5%)
  between operations  15.6 us (2%)
  starting transfers between devices  13.7 us (1%)
  loops' own time  9.77 us (1%)
    all_gather x2, waiting for transfers between devices, dispatch(): return lax.all_gather(packed, 'hidden', axis=0, tiled=True)  137 us
    psum x1, waiting for transfers between devices, run(): flat = lax.psum(flat, ('expert', 'hidden'))  131 us
    reduce_scatter x2, waiting for transfers between devices, give_back(): lax.psum_scatter(partial, 'hidden', scatter_dimension=0, tiled=True)  110 us
    pallas_call x1, Pallas kernels, expert_rows(): pl.pallas_call(functools.partial(expert_kernel, experts), grid_spec=pltpu...  46.3 us
    pallas_call x1, Pallas kernels, expert_grads(): pl.pallas_call(expert_grad_kernel, grid_spec=pltpu.PrefetchScalarGridSpec...  43.1 us
    unnamed x1, blocking collectives  42 us
    all_to_all x1, blocking collectives, dispatch(): lax.all_to_all(slots.reshape(expert_devs, chunk, width), 'expert', 0, 0,...  40.5 us
    all_to_all x2, waiting for transfers between devices, give_back(): lax.all_to_all(slots.reshape(expert_devs, chunk, width), 'expert', 0, 0,...  40.2 us
  transfers between devices with their start and end apart: 8, of which 7 were waited for; matrix products, arithmetic and copies ran while one was open for 20% of the time, Pallas kernels for 5%

profile of v1, /device:TPU:0, one launch (start us, length us, event | category | flops | bytes accessed | tf_op | source)
XLA Modules:
  0.0 905.5 jit_solution(7154269657686159492)
XLA Ops:
  7.9 3.1 gather_fusion
  11.4 42.0 %all-reduce = s32[512]{0:T(512)S(1)} all-reduce(s32[512]{0:T(512)S(1)} %dynamic-update-slice), channel_id=2, replica_groups=mesh['expert'=8,'hidden'=4] {'expert','hidden'}, use_global_device_ids=true, to_apply=%add | all-reduce | flops 512 | bytes 4096
  56.2 835.9 %conditional.4 = (f32[512,1024]{1,0:T(8,128)}, f32[1024]{0:T(1024)}, f32[1024]{0:T(1024)}, f32[1024]{0:T(1024)}, f32[1024]{0:T(1024)}, /*index=5*/f32[2,1024,102...) conditional(s32[]{:T(128)} %clamp.27, (s32[8,2]{1,0:T(8,128)S(1)}, ...), branch_computations={%region_4.32_spmd, %region_32.60_spmd, %region_60.88_spmd} | conditional | flops 119341531136 | bytes 1046124736
  56.5 4.7 convolution_convert_fusion.2
  61.2 4.6 all-to-all-start.1
  67.6 36.1 %all-to-all-done.1 = bf16[8,192,1024]{2,1,0:T(8,128)(2,1)} async-done(((bf16[8,192,1024]{2,1,0:T(8,128)(2,1)}), bf16[8,192,1024]{2,1,0:T(8,128)(2,1)}, u32[]{:S(2)}, u32[]{:S(2)}) %all-to-all-start.1) | async-done | bytes 3145760 | tf_op jit(solution)/shard_map/cond/branch_0_fun/all_to_all | solution.py:239
  103.7 5.6 fusion.30
  109.4 7.8 convolution_convert_fusion.1
  117.2 4.9 copy.151
  122.2 9.9 %fusion.208 = (f32[16,512]{1,0:T(8,128)S(1)}, f32[16,512,512]{1,2,0:T(8,128)}) fusion(bf16[512,3,16,64]{0,3,2,1:T(8,128)(2,1)} %bitcast.293, pred[512,512]{0,1:T(8,128)(4,1)S(1)} %iota_compare_fusion.20), kind=kOutput, calls=%fused_computation.403 | convolution fusion | flops 549445632 | bytes 19169280 | tf_op jit(solution)/shard_map/cond/branch_0_fun/qhd,khd->hqk/dot_general | solution.py:27
  132.1 8.3 fusion
  140.4 9.3 %fusion.35 = bf16[16,64,512]{2,1,0:T(8,128)(2,1)S(1)} fusion(f32[16,512,512]{1,2,0:T(8,128)} %get-tuple-element.594, f32[16,512]{1,0:T(8,128)S(1)} %fusion, f32[16,512]{1,0:T(8,128)S(1)} %get-tuple-element.593, bf16[512,3,16,64]{0,3,2,1:T(8,128)(2,1)} %bitcast.294), kind=kOutput, calls=%fused_computation.64 | convolution fusion | flops 549978112 | bytes 18939904 | tf_op jit(solution)/shard_map/cond/branch_0_fun/hqk,khd->qhd/dot_general | solution.py:266
  151.5 2.0 convolution_convert_fusion.3
  153.6 40.5 %all_to_all.48 = bf16[8,192,1024]{2,1,0:T(8,128)(2,1)S(1)} all-to-all(bf16[8,192,1024]{2,1,0:T(8,128)(2,1)S(1)} %bitcast.334), channel_id=1, replica_groups=mesh['expert'=8,'hidden'=4] {'expert'}, dimensions={0} | all-to-all | bytes 6291456 | tf_op jit(solution)/shard_map/cond/branch_0_fun/all_to_all | solution.py:239
  194.1 3.7 fusion.29
  201.5 21.4 %all-gather.10.cloned.1.call-done.cot = bf16[3072,1024]{1,0:T(8,128)(2,1)} async-done(((bf16[768,1024]{1,0:T(8,128)(2,1)}), bf16[3072,1024]{1,0:T(8,128)(2,1)}) %all-gather.10.cloned.1.call-update) | async-done | bytes 6291472 | tf_op jit(solution)/shard_map/cond/branch_0_fun/all_gather | solution.py:245
  222.9 115.8 %all-gather.8.cloned.1.call-done.x = bf16[3072,1024]{1,0:T(8,128)(2,1)} async-done(((bf16[768,1024]{1,0:T(8,128)(2,1)}), bf16[3072,1024]{1,0:T(8,128)(2,1)}) %all-gather.8.cloned.1.call-update) | async-done | bytes 6291472 | tf_op jit(solution)/shard_map/cond/branch_0_fun/all_gather | solution.py:245
  338.7 46.3 %expert_rows.3 = (bf16[3072,1024]{1,0:T(8,128)(2,1)}, bf16[3072,1024]{1,0:T(8,128)(2,1)}, bf16[3072,1024]{1,0:T(8,128)(2,1)}, bf16[3072,1024]{1,0:T(8,128)(2,1)}) custom-call(s32[12,2]{1,0:T(8,128)} %stack.58.has, bf16[3072,1024]{1,0:T(8,128)(2,1)} %all-gather.8.cloned.1.call-done.x, bf16[3072,1024]{1,0:T(8,128)(2,1)} %all-gather.10.cloned.1.call-done.cot, ...), custom_call_target="tpu_custom_call" | custom-call | flops 25769803776 | bytes 46137344 | tf_op jit(solution)/shard_map/cond/branch_0_fun/expert_rows/pallas_call | solution.py:79
  385.0 109.8 %reduce-scatter.7.cloned.1.call-done = bf16[768,1024]{1,0:T(8,128)(2,1)} async-done(((bf16[3072,1024]{1,0:T(8,128)(2,1)}), bf16[768,1024]{1,0:T(8,128)(2,1)}) %reduce-scatter.7.cloned.1.call-update) | async-done | bytes 1572880 | tf_op jit(solution)/shard_map/cond/branch_0_fun/reduce_scatter | solution.py:248
  494.9 5.4 fusion.10
  500.3 4.4 all-to-all-start.2
  505.4 37.2 %all-to-all-done.2 = bf16[8,192,1024]{2,1,0:T(8,128)(2,1)} async-done(((bf16[8,192,1024]{2,1,0:T(8,128)(2,1)}), bf16[8,192,1024]{2,1,0:T(8,128)(2,1)}, u32[]{:S(2)}, u32[]{:S(2)}) %all-to-all-start.2) | async-done | bytes 3145760 | tf_op jit(solution)/shard_map/cond/branch_0_fun/all_to_all | solution.py:250
  542.6 4.2 multiply_reduce_fusion.1
  550.2 2.3 convolution_convert_fusion.5
  552.4 2.7 copy.154
  555.1 11.3 %multiply_reduce_fusion = (f32[16,512]{1,0:T(8,128)S(1)}, f32[16,512,512]{1,2,0:T(8,128)}) fusion(f32[16,512,512]{1,2,0:T(8,128)} %get-tuple-element.594, f32[16,512]{1,0:T(8,128)S(1)} %log_add_fusion, bf16[512,16,64]{0,2,1:T(8,128)(2,1)} %bitcast.308, bf16[512,3,16,64]{0,3,2,1:T(8,128)(2,1)S(1)} %bitcast.295), kind=kOutput, calls=%fused_computation.2 | convolution fusion | flops 549445632 | bytes 35717120 | tf_op jit(solution)/shard_map/cond/branch_0_fun/qhd,khd->hqk/dot_general | solution.py:293
  566.3 15.7 %multiply_convert_fusion = bf16[16,512,512]{1,2,0:T(8,128)(2,1)} fusion(f32[16,512,512]{1,2,0:T(8,128)} %get-tuple-element.599, f32[16,512,512]{1,2,0:T(8,128)} %get-tuple-element.594, f32[16,512]{1,0:T(8,128)S(1)} %get-tuple-element.598, f32[16,512]{1,0:T(8,128)S(1)} %log_add_fusion), kind=kLoop, calls=%fused_computation.1 | loop fusion | flops 16777216 | bytes 42008576 | tf_op jit(solution)/shard_map/cond/branch_0_fun/convert_element_type | solution.py:294
  582.1 7.8 fusion.40
  589.9 6.0 fusion.39
  595.9 5.0 fusion.41
  600.9 2.3 pad_maximum_fusion
  603.2 1.7 copy-done.43
  604.8 5.9 convolution_convert_fusion
  610.7 10.4 %reshape.1119 = bf16[3072,1024]{1,0:T(8,128)(2,1)} reshape(bf16[1024,3072]{1,0:T(8,128)(2,1)} %convolution_convert_fusion) | data formatting | bytes 12582912 | tf_op jit(solution)/shard_map/cond/branch_0_fun/reshape | solution.py:310
  621.2 7.0 fusion.28
  632.0 32.4 %concatenate.6 = bf16[4104,1024]{1,0:T(8,128)(2,1)} concatenate(bf16[3072,1024]{1,0:T(8,128)(2,1)} %reshape.1119, bf16[1024,1024]{1,0:T(8,128)(2,1)S(1)} %convolution_convert_fusion.4, bf16[4,1024]{1,0:T(4,128)(2,1)S(1)} %fusion.60, bf16[4,1024]{1,0:T(4,128)(2,1)S(1)} %subtract_convert_fusion), dimensions={0} | concatenate | bytes 16809984 | tf_op jit(solution)/shard_map/cond/branch_0_fun/concatenate | solution.py:308
  664.4 5.5 fusion.11
  669.9 4.5 all-to-all-start.3
  674.4 43.1 %expert_grads.3 = (f32[2,1024,1024]{2,1,0:T(8,128)}, f32[2,1024,1024]{2,1,0:T(8,128)}) custom-call(s32[12,2]{1,0:T(8,128)} %stack.58.has, bf16[3072,1024]{1,0:T(8,128)(2,1)} %all-gather.8.cloned.1.call-done.x, bf16[3072,1024]{1,0:T(8,128)(2,1)} %all-gather.10.cloned.1.call-done.cot, f32[3072,1]{1,0:T(8,128)} %bitcast.340, ...), custom_call_target="tpu_custom_call" | custom-call | flops 12884901888 | bytes 67108864 | tf_op jit(solution)/shard_map/cond/branch_0_fun/expert_grads/pallas_call | solution.py:130
  717.6 2.2 add_add_fusion.2
  719.8 3.0 all-to-all-done.3
  722.8 4.4 add_convert_fusion
  727.1 131.3 %all-reduce.5.cloned.1.call-done = bf16[4104,1024]{1,0:T(8,128)(2,1)} async-done(((bf16[4104,1024]{1,0:T(8,128)(2,1)}), bf16[4104,1024]{1,0:T(8,128)(2,1)}) %all-reduce.5.cloned.1.call-update) | async-done | bytes 8405008 | tf_op jit(solution)/shard_map/cond/branch_0_fun/psum | solution.py:316
  859.8 6.2 slice.191
  866.0 10.4 %reshape.1124 = bf16[1024,3072]{1,0:T(8,128)(2,1)} reshape(bf16[3072,1024]{1,0:T(8,128)(2,1)} %slice.191) | data formatting | bytes 12582912 | tf_op jit(solution)/shard_map/cond/branch_0_fun/reshape | solution.py:319
  876.4 4.4 reshape.1189
  880.8 2.0 slice_convert_fusion
  892.2 4.7 copy-done.35
  (143 shorter events, 20.9 us)
Async XLA Ops:
  7.2 0.8 copy-start
  61.2 5.7 copy-start.2
  61.2 42.5 %all-to-all-start.1 = ((bf16[8,192,1024]{2,1,0:T(8,128)(2,1)}), bf16[8,192,1024]{2,1,0:T(8,128)(2,1)}, u32[]{:S(2)}, u32[]{:S(2)}) async-start(bf16[8,192,1024]{2,1,0:T(8,128)(2,1)} %bitcast.316), calls=%async_computation.1 | async-start | bytes 6291456 | tf_op jit(solution)/shard_map/cond/branch_0_fun/all_to_all | solution.py:239
  65.8 157.1 %all-gather.10.cloned.1.call-start = ((), (), s32[]{:S(2)}) async-start(), calls=%async_computation.19 | async-start | bytes 7864320 | tf_op jit(solution)/shard_map/cond/branch_0_fun/all_gather | solution.py:245
  67.5 41.8 %copy-start.69 = (f32[512]{0:T(512)}, f32[512]{0:T(512)S(1)}, u32[]{:S(2)}) copy-start(f32[512]{0:T(512)S(1)} %fusion.27) | copy-start | bytes 6148
  103.7 5.7 copy-start.58
  103.7 5.7 copy-start.75
  109.3 229.4 %all-gather.8.cloned.1.call-start = ((), (), s32[]{:S(2)}) async-start(), calls=%async_computation.18 | async-start | bytes 7864320 | tf_op jit(solution)/shard_map/cond/branch_0_fun/all_gather | solution.py:245
  140.4 9.3 %copy-start.26 = (bf16[1024,1024]{1,0:T(8,128)(2,1)S(1)}, bf16[1024,1024]{1,0:T(8,128)(2,1)}, u32[]{:S(2)}) copy-start(bf16[1024,1024]{1,0:T(8,128)(2,1)} %get-tuple-element.223) | copy-start | bytes 6291460
  149.7 1.4 copy-start.46
  149.7 1.8 copy-start.62
  149.7 1.8 copy-start.79
  151.1 395.7 %copy-start.32 = (f32[512,1024]{1,0:T(8,128)}, f32[512,1024]{1,0:T(8,128)S(1)}, u32[]{:S(2)}) copy-start(f32[512,1024]{1,0:T(8,128)S(1)} %get-tuple-element.596) | copy-start | bytes 6291460
  197.8 297.0 %reduce-scatter.7.cloned.1.call-start = ((), (), s32[]{:S(2)}) async-start(), calls=%async_computation.20 | async-start | bytes 7864320 | tf_op jit(solution)/shard_map/cond/branch_0_fun/reduce_scatter | solution.py:248
  500.3 42.3 %all-to-all-start.2 = ((bf16[8,192,1024]{2,1,0:T(8,128)(2,1)}), bf16[8,192,1024]{2,1,0:T(8,128)(2,1)}, u32[]{:S(2)}, u32[]{:S(2)}) async-start(bf16[8,192,1024]{2,1,0:T(8,128)(2,1)} %bitcast.322), calls=%async_computation.3 | async-start | bytes 6291456 | tf_op jit(solution)/shard_map/cond/branch_0_fun/all_to_all | solution.py:250
  504.8 159.7 %reduce-scatter.9.cloned.1.call-start = ((), (), s32[]{:S(2)}) async-start(), calls=%async_computation.22 | async-start | bytes 7864320 | tf_op jit(solution)/shard_map/cond/branch_0_fun/reduce_scatter | solution.py:248
  505.3 353.1 %all-reduce.5.cloned.1.call-start = ((), (), s32[]{:S(2)}) async-start(), calls=%async_computation.21 | async-start | bytes 16809984 | tf_op jit(solution)/shard_map/cond/branch_0_fun/psum | solution.py:316
  546.8 1.2 copy-start.8
  547.6 1.3 copy-start.20
  547.6 2.6 copy-start.27
  548.9 1.0 copy-start.52
  550.1 4.9 copy-start.14
  566.3 29.5 %slice-start = ((s8[16777216]{0:T(1024)(128)(4,1)}), s8[4194304]{0:T(1024)(128)(4,1)S(1)}, s32[]{:S(2)}) async-start(s8[16777216]{0:T(1024)(128)(4,1)} %bitcast.287), calls=%async_computation.33 | async-start | bytes 8388608
  566.3 29.5 %slice-start.1 = ((s8[16777216]{0:T(1024)(128)(4,1)}), s8[4194304]{0:T(1024)(128)(4,1)S(1)}, s32[]{:S(2)}) async-start(s8[16777216]{0:T(1024)(128)(4,1)} %bitcast.287), calls=%async_computation.34 | async-start | bytes 8388608
  566.3 29.5 %slice-start.2 = ((s8[16777216]{0:T(1024)(128)(4,1)}), s8[4194304]{0:T(1024)(128)(4,1)S(1)}, s32[]{:S(2)}) async-start(s8[16777216]{0:T(1024)(128)(4,1)} %bitcast.287), calls=%async_computation.35 | async-start | bytes 8388608
  582.1 7.8 copy-start.15
  589.9 6.0 slice-start.3
  600.9 4.0 copy-start.3
  603.2 1.7 copy-start.43
  621.2 7.0 copy-start.70
  628.1 1.4 copy-start.36
  628.1 2.6 copy-start.47
  628.1 2.6 copy-start.53
  669.9 52.9 %all-to-all-start.3 = ((bf16[8,192,1024]{2,1,0:T(8,128)(2,1)}), bf16[8,192,1024]{2,1,0:T(8,128)(2,1)}, u32[]{:S(2)}, u32[]{:S(2)}) async-start(bf16[8,192,1024]{2,1,0:T(8,128)(2,1)} %bitcast.319), calls=%async_computation.5 | async-start | bytes 6291456 | tf_op jit(solution)/shard_map/cond/branch_0_fun/all_to_all | solution.py:250
  674.4 43.1 %copy-start.9 = (bf16[512,1024]{1,0:T(8,128)(2,1)S(1)}, bf16[512,1024]{1,0:T(8,128)(2,1)}, u32[]{:S(2)}) copy-start(bf16[512,1024]{1,0:T(8,128)(2,1)} %get-tuple-element.226) | copy-start | bytes 3145732
  674.4 43.1 %copy-start.21 = (f32[512,1024]{1,0:T(8,128)S(1)}, f32[512,1024]{1,0:T(8,128)}, u32[]{:S(2)}) copy-start(f32[512,1024]{1,0:T(8,128)} %copy-done.20) | copy-start | bytes 6291460
  674.4 43.1 %copy-start.37 = (f32[512,1024]{1,0:T(8,128)S(1)}, f32[512,1024]{1,0:T(8,128)}, u32[]{:S(2)}) copy-start(f32[512,1024]{1,0:T(8,128)} %copy-done.36) | copy-start | bytes 6291460
  892.1 4.8 copy-start.35
  892.1 6.1 copy-start.42
  892.2 6.3 copy-start.82
  892.2 6.3 copy-start.1
Sparse Core Ops, SparseCore 0:
  109.4 113.4 all-gather.9
  225.1 113.5 all-gather.7
  385.1 109.6 reduce-scatter.6
  508.3 111.7 reduce-scatter.8
  664.5 193.8 all-reduce.4
